TPU v7x, 32 devices: a whole 2x2x4 slice. The times are simulated.
32 devices in a mesh: rows: 8 (over z, x), sk: 4 (over y, core).
Axes of the slice: x: 2, y: 2, z: 4, core: 2. Of those that a mesh axis runs over, the one named last changes fastest.
Arguments:
- panel: float32 [64, 262144], P(None, ('rows', 'sk')), may hold values from -200 to 200
- signs: int32 [262144], P(('rows', 'sk')), may hold values from -1 to 1
- sample_device: int32 [4096, 1], replicated, may hold values from 0 to 31; in each aligned block of 128 rows (0 to 127, 128 to 255, ...) at most 4 rows name the same one
- sample_offset: int32 [4096], replicated, may hold values from 0 to 8191
Outputs:
- mixed: float32 [64, 262144], P(None, ('rows', 'sk'))
- r_factor: float32 [64, 64], replicated
- whitened: float32 [64, 4096], P(None, ('rows', 'sk'))
Inputs may be any that keep to these rules, and one draw needn't show every extreme that they name: `sample_device`: among the sample positions j * 128 to (j + 1) * 128 - 1 of any j, no device number appears more than 4 times, and some block reaches it.
All inputs are finite; a program needn't handle non-finite values.
Results may differ from a plain program's by a relative error of at most 0.0003.
Values sent between devices are 32-bit elements; how exact they have to be, the bound alone decides.
No kernel may reach another device: no remote copies, remote signals or barrier semaphores. Data moves between devices by JAX's collectives and lax.ppermute only.
A program may use at most 64 MiB of HBM per device.

v0:
```python
import functools
import math

import jax
import jax.numpy as jnp
import numpy as np
from jax import lax
from jax.experimental import pallas as pl
from jax.experimental.pallas import tpu as pltpu
from jax.sharding import PartitionSpec as P

AXES = ("rows", "sk")
LANES = 128
GROUP = 16
SLICES = 6


def hadamard_table(order_size):
    shape = (order_size, order_size)
    common = lax.broadcasted_iota(jnp.int32, shape, 0) & lax.broadcasted_iota(jnp.int32, shape, 1)
    for distance in (4, 2, 1):
        common = common ^ (common >> distance)
    return (1 - 2 * (common & 1)).astype(jnp.float32).astype(jnp.bfloat16)


def whole(value):
    return pl.BlockSpec(value.shape, lambda i: (0,) * len(value.shape))


def in_hbm(value):
    return pltpu.with_memory_space_constraint(value, pltpu.HBM)


def mix_kernel(scale, panel_ref, signs_ref, out_ref):
    cols, rows = panel_ref.shape
    inner = rows // LANES
    width = out_ref.shape[2]
    step = min(width, LANES)
    table = hadamard_table(LANES)
    signs = signs_ref[...].astype(jnp.float32) * scale
    for first in range(0, cols, 8):
        flipped = panel_ref[first : first + 8, :] * signs
        stacked = jnp.concatenate(
            [flipped[:, a * LANES : (a + 1) * LANES] for a in range(inner)], axis=0
        )
        total = None
        rest = stacked
        for piece in range(3):
            part = rest.astype(jnp.bfloat16)
            term = jnp.dot(part, table, preferred_element_type=jnp.float32)
            total = term if total is None else total + term
            if piece < 2:
                rest = rest - part.astype(jnp.float32)
        blocks = [total[a * 8 : (a + 1) * 8] for a in range(inner)]
        span = 1
        while span < inner:
            for a in range(inner):
                if a & span == 0:
                    left, right = blocks[a], blocks[a + span]
                    blocks[a], blocks[a + span] = left + right, left - right
            span *= 2
        for start in range(0, rows, step):
            block = blocks[start // LANES][:, start % LANES : start % LANES + step]
            out_ref[start // width, first : first + 8, start % width : start % width + step] = block


def local_mix(panel, signs_row, scale, peers):
    cols, rows = panel.shape
    width = rows // peers
    return pl.pallas_call(
        functools.partial(mix_kernel, scale),
        grid=(cols // GROUP,),
        in_specs=[
            pl.BlockSpec((GROUP, rows), lambda i: (i, 0)),
            pl.BlockSpec((1, rows), lambda i: (0, 0)),
        ],
        out_specs=pl.BlockSpec((peers, GROUP, width), lambda i: (0, i, 0)),
        out_shape=pltpu.HBM((peers, cols, width), jnp.float32),
        compiler_params=pltpu.CompilerParams(vmem_limit_bytes=32 << 20),
    )(in_hbm(panel), in_hbm(signs_row))


def across_kernel(in_ref, token_ref, out_ref):
    del token_ref
    peers = in_ref.shape[0]
    step = min(in_ref.shape[2], LANES)
    for lane in range(0, in_ref.shape[2], step):
        for first in range(0, in_ref.shape[1], 8):
            columns = pl.ds(first, 8)
            blocks = [in_ref[p, columns, lane : lane + step] for p in range(peers)]
            span = 1
            while span < peers:
                for p in range(peers):
                    if p & span == 0:
                        left, right = blocks[p], blocks[p + span]
                        blocks[p], blocks[p + span] = left + right, left - right
                span *= 2
            for p in range(peers):
                out_ref[p, columns, lane : lane + step] = blocks[p]


def mix_across(received, token):
    peers, cols, width = received.shape
    spec = pl.BlockSpec((peers, GROUP, width), lambda i: (0, i, 0))
    return pl.pallas_call(
        across_kernel,
        grid=(cols // GROUP,),
        in_specs=[spec, pl.BlockSpec((8, LANES), lambda i: (0, 0))],
        out_specs=spec,
        out_shape=pltpu.HBM(received.shape, jnp.float32),
        compiler_params=pltpu.CompilerParams(vmem_limit_bytes=32 << 20),
    )(received, token)


def lay_out_kernel(in_ref, out_ref):
    peers, _, width = in_ref.shape
    for p in range(peers):
        out_ref[:, p * width : (p + 1) * width] = in_ref[p]


def lay_out(received):
    peers, cols, width = received.shape
    return pl.pallas_call(
        lay_out_kernel,
        grid=(cols // GROUP,),
        in_specs=[pl.BlockSpec((peers, GROUP, width), lambda i: (0, i, 0))],
        out_specs=pl.BlockSpec((GROUP, peers * width), lambda i: (i, 0)),
        out_shape=jax.ShapeDtypeStruct((cols, peers * width), jnp.float32),
        compiler_params=pltpu.CompilerParams(vmem_limit_bytes=32 << 20),
    )(received)


def terms_kernel(bits, half, code_ref, me_ref, far_ref, out_ref, mix_ref, table_ref, done_sem):
    peers, _, width = mix_ref.shape
    pieces = [
        pltpu.make_async_copy(far_ref.at[part], mix_ref.at[part], done_sem.at[number])
        for number, part in enumerate([pl.ds(0, peers // 2), pl.ds(peers // 2, peers // 2)])
    ]
    for piece in pieces:
        piece.start()
    rows = peers * width
    me = me_ref[0]

    span = max(1, LANES // width)

    def transpose_block(number, carry):
        p = number * span
        for lane in range(0, max(width, LANES), LANES):
            start = pl.multiple_of(p * width + lane, LANES)
            tile = jnp.concatenate(
                [mix_ref[p + i, :, lane : lane + min(width, LANES)] for i in range(span)], axis=1
            )
            turned = jnp.concatenate([tile, tile], axis=0).T
            table_ref[pl.ds(start, LANES), :] = turned
            table_ref[pl.ds(rows + start, LANES), :] = -turned
        return carry

    for number, piece in enumerate(pieces):
        piece.wait()
        count = peers // 2 // span
        lax.fori_loop(number * count, (number + 1) * count, transpose_block, 0)
    first_half = lax.broadcasted_iota(jnp.int32, (1, LANES), 1) < LANES // 2

    def gather_block(r, carry):
        mask = jnp.int32(0)
        for bit in range(bits):
            mask = mask | (((r >> bit) & 1) << (bits - 1 - bit))
        source = (me ^ mask) * (2 * half)
        target = pl.multiple_of(r * half, half)
        for j in range(half):
            upper = table_ref[pl.ds(code_ref[source + j], 1), :]
            lower = table_ref[pl.ds(code_ref[source + half + j], 1), :]
            out_ref[pl.ds(target + j, 1), :] = jnp.where(first_half, upper, lower)
        return carry

    lax.fori_loop(0, 1 << bits, gather_block, 0)


def sampled_terms(mix, code, me, bits, half):
    rows = mix.shape[0] * mix.shape[2]
    count = half << bits
    return pl.pallas_call(
        functools.partial(terms_kernel, bits, half),
        in_specs=[pl.BlockSpec(memory_space=pltpu.SMEM)] * 2
        + [pl.BlockSpec(memory_space=pltpu.HBM)],
        out_specs=pl.BlockSpec(memory_space=pltpu.VMEM),
        out_shape=jax.ShapeDtypeStruct((count, LANES), jnp.float32),
        scratch_shapes=[
            pltpu.VMEM(mix.shape, jnp.float32),
            pltpu.VMEM((2 * rows, LANES), jnp.float32),
            pltpu.SemaphoreType.DMA((2,)),
        ],
        compiler_params=pltpu.CompilerParams(vmem_limit_bytes=40 << 20),
        cost_estimate=pl.CostEstimate(
            flops=count * LANES * 40, bytes_accessed=24 << 20, transcendentals=0
        ),
    )(code, me, in_hbm(mix))


def two_sum(a, b):
    total = a + b
    part = total - a
    return total, (a - (total - part)) + (b - part)


def quick_sum(a, b):
    total = a + b
    return total, b - (total - a)


def pair_add(a, b):
    total, error = two_sum(a[0], b[0])
    return quick_sum(total, error + (a[1] + b[1]))


def halves(a):
    scaled = a * 4097.0
    high = scaled - (scaled - a)
    return high, a - high


def product(a, b, a_parts, b_parts):
    whole = a * b
    error = (a_parts[0] * b_parts[0] - whole) + a_parts[0] * b_parts[1]
    error = (error + a_parts[1] * b_parts[0]) + a_parts[1] * b_parts[1]
    return whole, error


def gram_kernel(scale, terms_ref, picked_ref, gram_ref):
    cols = picked_ref.shape[0]
    turned = terms_ref[...].T
    picked = jnp.concatenate([turned[:cols], turned[cols:]], axis=1)
    picked_ref[...] = picked
    rest = picked * scale
    shift = jnp.max(jnp.abs(rest), axis=1, keepdims=True) * float(1 << 17)
    parts = []
    for _ in range(SLICES):
        part = (rest + shift) - shift
        rest = rest - part
        shift = shift * (1.0 / 64.0)
        parts.append(part.astype(jnp.bfloat16))
    total = None
    for level in range(SLICES):
        left = jnp.concatenate(parts[: level + 1], axis=1)
        right = jnp.concatenate(parts[: level + 1][::-1], axis=1)
        term = lax.dot_general(
            left, right, (((1,), (1,)), ((), ())), preferred_element_type=jnp.float32
        )
        if total is None:
            total = (term, jnp.zeros_like(term))
        else:
            high, error = two_sum(total[0], term)
            total = (high, total[1] + error)
    high, low = quick_sum(*total)
    gram_ref[...] = jnp.concatenate([high, low], axis=1)


def own_gram(terms, cols, per_device, scale):
    return pl.pallas_call(
        functools.partial(gram_kernel, scale),
        grid=(1,),
        in_specs=[whole(terms)],
        out_specs=(
            pl.BlockSpec((cols, per_device), lambda i: (0, 0)),
            pl.BlockSpec((cols, 2 * cols), lambda i: (0, 0)),
        ),
        out_shape=(
            jax.ShapeDtypeStruct((cols, per_device), jnp.float32),
            jax.ShapeDtypeStruct((cols, 2 * cols), jnp.float32),
        ),
        compiler_params=pltpu.CompilerParams(vmem_limit_bytes=8 << 20),
    )(terms)


def tree_sum(values):
    while len(values) > 1:
        values = [pair_add(values[i], values[i + 1]) for i in range(0, len(values), 2)]
    return values[0]


def split_pair(packed):
    cols = packed.shape[0]
    return packed[:, :cols], packed[:, cols:]


def gram_sum_kernel(count, *refs):
    high, low = tree_sum([split_pair(ref[...]) for ref in refs[:count]])
    refs[-1][...] = jnp.concatenate([high, low], axis=1)


def gram_sum(grams, *through):
    count = len(grams)
    in_place = pl.BlockSpec(memory_space=pltpu.HBM)
    return pl.pallas_call(
        functools.partial(gram_sum_kernel, count),
        grid=(1,),
        in_specs=[whole(gram) for gram in grams] + [in_place] * len(through),
        out_specs=tuple([in_place] * len(through) + [whole(grams[0])]),
        out_shape=tuple(
            [pltpu.HBM(v.shape, v.dtype) for v in through]
            + [jax.ShapeDtypeStruct(grams[0].shape, jnp.float32)]
        ),
        input_output_aliases={count + i: i for i in range(len(through))},
        compiler_params=pltpu.CompilerParams(vmem_limit_bytes=8 << 20),
    )(*grams, *through)


def factor_kernel(picked_ref, *refs):
    gram_refs, (r_ref, white_ref) = refs[:-2], refs[-2:]
    cols = r_ref.shape[0]
    high, low = tree_sum([split_pair(ref[...]) for ref in gram_refs])
    row_id = lax.broadcasted_iota(jnp.int32, (cols, cols), 0)
    lane_id = lax.broadcasted_iota(jnp.int32, (cols, cols), 1)
    unit = (row_id == lane_id).astype(jnp.float32)
    wide_high = jnp.concatenate([high, unit], axis=1)
    wide_low = jnp.concatenate([low, jnp.zeros_like(unit)], axis=1)
    tiles = cols // 8
    shape = (8, 2 * cols)
    rows = [
        (wide_high[t * 8 : (t + 1) * 8], wide_low[t * 8 : (t + 1) * 8])
        for t in range(tiles)
    ]
    sub_id = lax.broadcasted_iota(jnp.int32, shape, 0)
    for j in range(cols - 1):
        tile, sub = divmod(j, 8)
        row = [jnp.broadcast_to(v[sub : sub + 1], shape) for v in rows[tile]]
        pivot = [jnp.broadcast_to(v[sub : sub + 1, j : j + 1], shape) for v in rows[tile]]
        first = 1.0 / pivot[0]
        first_parts = halves(first)
        whole, error = product(pivot[0], first, halves(pivot[0]), first_parts)
        gap = ((1.0 - whole) - error) - pivot[1] * first
        inverse = quick_sum(first, first * gap)
        whole, error = product(row[0], inverse[0], halves(row[0]), halves(inverse[0]))
        scaled = quick_sum(whole, error + (row[0] * inverse[1] + row[1] * inverse[0]))
        scaled_parts = halves(scaled[0])
        for t in range(tile, tiles):
            if t == tile and sub == 7:
                continue
            high, low = rows[t]
            column = [jnp.broadcast_to(v[:, j : j + 1], shape) for v in rows[t]]
            if t == tile:
                column = [jnp.where(sub_id > sub, v, 0.0) for v in column]
            whole, error = product(column[0], scaled[0], halves(column[0]), scaled_parts)
            error = error + (column[0] * scaled[1] + column[1] * scaled[0])
            total, missed = two_sum(high, -whole)
            rows[t] = quick_sum(total, missed + (low - error))
    wide_high = jnp.concatenate([v[0] for v in rows], axis=0)
    wide_low = jnp.concatenate([v[1] for v in rows], axis=0)
    wide_row = lax.broadcasted_iota(jnp.int32, wide_high.shape, 0)
    wide_lane = lax.broadcasted_iota(jnp.int32, wide_high.shape, 1)
    diagonal = jnp.sum(jnp.where(wide_row == wide_lane, wide_high, 0.0), axis=1, keepdims=True)
    root = jnp.sqrt(diagonal)
    wide = (wide_high + wide_low) / root
    r_ref[...] = jnp.where(lane_id >= row_id, wide[:, :cols], 0.0)
    white_ref[...] = jnp.dot(
        wide[:, cols:],
        picked_ref[...],
        precision=lax.Precision.HIGHEST,
        preferred_element_type=jnp.float32,
    )


def factor_and_solve(picked, grams):
    cols = picked.shape[0]
    return pl.pallas_call(
        factor_kernel,
        grid=(1,),
        in_specs=[whole(value) for value in (picked, *grams)],
        out_specs=(pl.BlockSpec((cols, cols), lambda i: (0, 0)), whole(picked)),
        out_shape=(
            jax.ShapeDtypeStruct((cols, cols), jnp.float32),
            jax.ShapeDtypeStruct(picked.shape, jnp.float32),
        ),
        compiler_params=pltpu.CompilerParams(vmem_limit_bytes=8 << 20),
    )(picked, *grams)


def xor_permute(value, mask, device_count):
    return lax.ppermute(value, AXES, [(i, i ^ mask) for i in range(device_count)])


def in_groups(masks, size=2):
    odd = len(masks) % size
    groups = [masks[:odd]] if odd else []
    return groups + [masks[i : i + size] for i in range(odd, len(masks), size)]


def combined(masks, q):
    mask = 0
    for bit, value in enumerate(masks):
        if (q >> bit) & 1:
            mask |= value
    return mask


def local(panel, signs, sample_device, sample_offset):
    device_count = lax.axis_size(AXES)
    me = lax.axis_index(AXES).astype(jnp.int32)
    bits = device_count.bit_length() - 1
    cols, rows = panel.shape
    samples = sample_offset.shape[0]
    per_device = samples // device_count
    half = per_device // 2
    masks = [1 << bit for bit in range(bits)]

    signs_row = signs.reshape(1, rows)
    scale = 1.0 / math.sqrt(rows * device_count)

    mix = local_mix(panel, signs_row, scale, device_count)

    def swap(value):
        return lax.all_to_all(value, AXES, split_axis=0, concat_axis=0, tiled=True)

    received_mix = swap(mix)

    common = me & sample_device[:, 0]
    odd = lax.population_count(common) & 1
    code = sample_offset + odd * rows
    total = sampled_terms(mix, code, me.reshape(1), bits, half)
    for group in in_groups(masks):
        block = total.shape[0] >> len(group)
        mine = total[:block]
        for q in range(1, 1 << len(group)):
            mask = combined(group[::-1], q)
            sent = total[q * block : (q + 1) * block]
            mine = mine + xor_permute(sent, mask, device_count)
        total = mine
    picked, gram = own_gram(total, cols, per_device, 1.0 / math.sqrt(samples))
    across = mix_across(received_mix, gram)
    groups = in_groups(masks)[::-1]
    for number, group in enumerate(groups):
        received = [gram] + [
            xor_permute(gram, combined(group, q), device_count) for q in range(1, 1 << len(group))
        ]
        if number == 0:
            across, gram = gram_sum(received, across)
            mixed = lay_out(swap(across))
        elif number < len(groups) - 1:
            (gram,) = gram_sum(received)
    r_factor, whitened = factor_and_solve(picked, received)
    return (mixed, r_factor, whitened)


def solution(mesh):
    return jax.shard_map(
        local,
        mesh=mesh,
        in_specs=(P(None, AXES), P(AXES), P(), P()),
        out_specs=(P(None, AXES), P(), P(None, AXES)),
        check_vma=False,
    )
```

profile of v0, /device:TPU:0, one launch (start us, length us, event | category | flops | bytes accessed | tf_op | source)
XLA Modules:
  0.0 127.6 jit_solution(3173995812554654116)
XLA Ops:
  0.6 4.6 %shard_map.67.far_ref = f32[32,64,256]{2,1,0:T(8,128)} custom-call(f32[64,8192]{1,0:T(8,128)} %panel_ref.1, s32[1,8192]{1,0:T(1,128)} %bitcast.4), custom_call_target="tpu_custom_call" | custom-call | tf_op jit(solution)/shard_map/pallas_call | solution.py:70
  5.3 7.3 %all-to-all-start = ((f32[32,64,256]{2,1,0:T(8,128)}), f32[32,64,256]{2,1,0:T(8,128)S(1)}, u32[]{:S(2)}, u32[]{:S(2)}) async-start(f32[32,64,256]{2,1,0:T(8,128)} %shard_map.67.far_ref), calls=%async_computation | async-start | bytes 4194304 | tf_op jit(solution)/shard_map/all_to_all | solution.py:412
  12.6 8.8 %shard_map.68 = f32[2048,128]{1,0:T(8,128)S(1)} custom-call(s32[4096]{0:T(1024)S(1)} %add.28.code_ref, s32[1]{0:T(128)} %bitcast.1.me_ref, f32[32,64,256]{2,1,0:T(8,128)} %shard_map.67.far_ref), custom_call_target="tpu_custom_call" | custom-call | flops 10485760 | bytes 25165824 | tf_op jit(solution)/shard_map/pallas_call | solution.py:182
  21.8 1.7 %collective-permute-done = f32[1024,128]{1,0:T(8,128)S(1)} collective-permute-done((f32[1024,128]{1,0:T(8,128)S(1)}, f32[1024,128]{1,0:T(8,128)S(1)}, u32[]{:S(2)}, u32[]{:S(2)}) %collective-permute-start) | collective-permute-done | bytes 524320 | tf_op jit(solution)/shard_map/ppermute | solution.py:379
  23.6 1.8 %collective-permute-start.1 = (f32[256,128]{1,0:T(8,128)S(1)}, f32[256,128]{1,0:T(8,128)S(1)}, u32[]{:S(2)}, u32[]{:S(2)}) collective-permute-start(f32[256,128]{1,0:T(8,128)S(1)} %get-tuple-element.15), channel_id=1, source_target_pairs={{0,4},{1,5},{2,6},{3,7},{4,0},{5,1},{6,2},{7,3},{8,12},{9,13},{10,... | collective-permute-start | bytes 393224 | tf_op jit(solution)/shard_map/ppermute | solution.py:379
  25.4 1.5 %collective-permute-start.2 = (f32[256,128]{1,0:T(8,128)S(1)}, f32[256,128]{1,0:T(8,128)S(1)}, u32[]{:S(2)}, u32[]{:S(2)}) collective-permute-start(f32[256,128]{1,0:T(8,128)S(1)} %get-tuple-element.17), channel_id=1, source_target_pairs={{0,2},{1,3},{2,0},{3,1},{4,6},{5,7},{6,4},{7,5},{8,10},{9,11},{10,... | collective-permute-start | bytes 393224 | tf_op jit(solution)/shard_map/ppermute | solution.py:379
  27.1 6.7 %collective-permute-done.1 = f32[256,128]{1,0:T(8,128)S(1)} collective-permute-done((f32[256,128]{1,0:T(8,128)S(1)}, f32[256,128]{1,0:T(8,128)S(1)}, u32[]{:S(2)}, u32[]{:S(2)}) %collective-permute-start.1) | collective-permute-done | bytes 131104 | tf_op jit(solution)/shard_map/ppermute | solution.py:379
  33.9 7.9 %collective-permute-done.3 = f32[256,128]{1,0:T(8,128)S(1)} collective-permute-done((f32[256,128]{1,0:T(8,128)S(1)}, f32[256,128]{1,0:T(8,128)S(1)}, u32[]{:S(2)}, u32[]{:S(2)}) %collective-permute-start.3) | collective-permute-done | bytes 131104 | tf_op jit(solution)/shard_map/ppermute | solution.py:379
  41.9 1.7 %collective-permute-start.5 = (f32[64,128]{1,0:T(8,128)S(1)}, f32[64,128]{1,0:T(8,128)S(1)}, u32[]{:S(2)}, u32[]{:S(2)}) collective-permute-start(f32[64,128]{1,0:T(8,128)S(1)} %get-tuple-element.20), channel_id=1, source_target_pairs={{0,8},{1,9},{2,10},{3,11},{4,12},{5,13},{6,14},{7,15},{8,0},{9,1},... | collective-permute-start | bytes 98312 | tf_op jit(solution)/shard_map/ppermute | solution.py:379
  43.5 2.7 %collective-permute-start.6 = (f32[64,128]{1,0:T(8,128)S(1)}, f32[64,128]{1,0:T(8,128)S(1)}, u32[]{:S(2)}, u32[]{:S(2)}) collective-permute-start(f32[64,128]{1,0:T(8,128)S(1)} %get-tuple-element.19), channel_id=1, source_target_pairs={{0,24},{1,25},{2,26},{3,27},{4,28},{5,29},{6,30},{7,31},{8,16},{9,... | collective-permute-start | bytes 98312 | tf_op jit(solution)/shard_map/ppermute | solution.py:379
  46.3 17.5 %collective-permute-done.4 = f32[64,128]{1,0:T(8,128)S(1)} collective-permute-done((f32[64,128]{1,0:T(8,128)S(1)}, f32[64,128]{1,0:T(8,128)S(1)}, u32[]{:S(2)}, u32[]{:S(2)}) %collective-permute-start.4) | collective-permute-done | bytes 32800 | tf_op jit(solution)/shard_map/ppermute | solution.py:379
  64.4 1.0 collective-permute-start.7
  66.2 2.6 %collective-permute-start.9 = (f32[64,128]{1,0:T(8,128)S(1)}, f32[64,128]{1,0:T(8,128)S(1)}, u32[]{:S(2)}, u32[]{:S(2)}) collective-permute-start(f32[64,128]{1,0:T(8,128)S(1)} %get-tuple-element.9.token_ref.refs_0_), channel_id=1, source_target_pairs={{0,24},{1,25},{2,26},{3,27},{4,28},{5,29},{6,30},{7,31},{8,16},{9,... | collective-permute-start | bytes 98312 | tf_op jit(solution)/shard_map/ppermute | solution.py:379
  68.8 2.2 %shard_map.70.refs_4_ = f32[32,64,256]{2,1,0:T(8,128)} custom-call(f32[32,64,256]{2,1,0:T(8,128)S(1)} %all-to-all-done.in_ref, f32[64,128]{1,0:T(8,128)S(1)} %get-tuple-element.9.token_ref.refs_0_), custom_call_target="tpu_custom_call" | custom-call | tf_op jit(solution)/shard_map/pallas_call | solution.py:105
  71.0 0.9 collective-permute-done.9.refs_3_
  72.1 4.8 %all-to-all-start.1 = ((f32[32,64,256]{2,1,0:T(8,128)}), f32[32,64,256]{2,1,0:T(8,128)S(1)}, u32[]{:S(2)}, u32[]{:S(2)}) async-start(f32[32,64,256]{2,1,0:T(8,128)} %get-tuple-element.10), calls=%async_computation.1 | async-start | bytes 4194304 | tf_op jit(solution)/shard_map/all_to_all | solution.py:412
  76.9 1.8 %collective-permute-start.10 = (f32[64,128]{1,0:T(8,128)S(1)}, f32[64,128]{1,0:T(8,128)S(1)}, u32[]{:S(2)}, u32[]{:S(2)}) collective-permute-start(f32[64,128]{1,0:T(8,128)S(1)} %get-tuple-element.12.refs_0_), channel_id=1, source_target_pairs={{0,2},{1,3},{2,0},{3,1},{4,6},{5,7},{6,4},{7,5},{8,10},{9,11},{10,... | collective-permute-start | bytes 98312 | tf_op jit(solution)/shard_map/ppermute | solution.py:379
  78.7 1.5 %collective-permute-start.11 = (f32[64,128]{1,0:T(8,128)S(1)}, f32[64,128]{1,0:T(8,128)S(1)}, u32[]{:S(2)}, u32[]{:S(2)}) collective-permute-start(f32[64,128]{1,0:T(8,128)S(1)} %get-tuple-element.12.refs_0_), channel_id=1, source_target_pairs={{0,4},{1,5},{2,6},{3,7},{4,0},{5,1},{6,2},{7,3},{8,12},{9,13},{10,... | collective-permute-start | bytes 98312 | tf_op jit(solution)/shard_map/ppermute | solution.py:379
  80.5 4.3 %collective-permute-done.10.refs_1_ = f32[64,128]{1,0:T(8,128)S(1)} collective-permute-done((f32[64,128]{1,0:T(8,128)S(1)}, f32[64,128]{1,0:T(8,128)S(1)}, u32[]{:S(2)}, u32[]{:S(2)}) %collective-permute-start.10) | collective-permute-done | bytes 32800 | tf_op jit(solution)/shard_map/ppermute | solution.py:379
  84.7 10.3 %collective-permute-done.11.refs_2_ = f32[64,128]{1,0:T(8,128)S(1)} collective-permute-done((f32[64,128]{1,0:T(8,128)S(1)}, f32[64,128]{1,0:T(8,128)S(1)}, u32[]{:S(2)}, u32[]{:S(2)}) %collective-permute-start.11) | collective-permute-done | bytes 32800 | tf_op jit(solution)/shard_map/ppermute | solution.py:379
  95.3 1.2 collective-permute-done.13.refs_1_
  96.5 11.7 %shard_map.74 = (f32[64,64]{1,0:T(8,128)}, f32[64,128]{1,0:T(8,128)}) custom-call(f32[64,128]{1,0:T(8,128)S(1)} %get-tuple-element.11.picked_ref, f32[64,128]{1,0:T(8,128)S(1)} %shard_map.73.refs_0_, f32[64,128]{1,0:T(8,128)S(1)} %collective-permute-done.13.refs_1_), custom_call_target="tpu_custom_call" | custom-call | tf_op jit(solution)/shard_map/pallas_call | solution.py:365
  108.2 17.5 %all-to-all-done.1.in_ref = f32[32,64,256]{2,1,0:T(8,128)S(1)} async-done(((f32[32,64,256]{2,1,0:T(8,128)}), f32[32,64,256]{2,1,0:T(8,128)S(1)}, u32[]{:S(2)}, u32[]{:S(2)}) %all-to-all-start.1) | async-done | bytes 2097184 | tf_op jit(solution)/shard_map/all_to_all | solution.py:412
  125.7 1.9 %shard_map.72 = f32[64,8192]{1,0:T(8,128)} custom-call(f32[32,64,256]{2,1,0:T(8,128)S(1)} %all-to-all-done.1.in_ref), custom_call_target="tpu_custom_call" | custom-call | tf_op jit(solution)/shard_map/pallas_call | solution.py:123
  (28 shorter events, 2.9 us)
Async XLA Ops:
  5.3 7.3 %copy-start.1 = (s32[4096,1]{0,1:T(1,128)S(1)}, s32[4096,1]{0,1:T(1,128)}, u32[]{:S(2)}) copy-start(s32[4096,1]{0,1:T(1,128)} %param.6) | copy-start | bytes 49156
  5.3 7.3 %copy-start = (s32[4096]{0:T(1024)S(1)}, s32[4096]{0:T(1024)}, u32[]{:S(2)}) copy-start(s32[4096]{0:T(1024)} %param.7) | copy-start | bytes 49156
  5.3 63.6 %all-to-all-start = ((f32[32,64,256]{2,1,0:T(8,128)}), f32[32,64,256]{2,1,0:T(8,128)S(1)}, u32[]{:S(2)}, u32[]{:S(2)}) async-start(f32[32,64,256]{2,1,0:T(8,128)} %shard_map.67.far_ref), calls=%async_computation | async-start | bytes 4194304 | tf_op jit(solution)/shard_map/all_to_all | solution.py:412
  21.5 2.0 %collective-permute-start = (f32[1024,128]{1,0:T(8,128)S(1)}, f32[1024,128]{1,0:T(8,128)S(1)}, u32[]{:S(2)}, u32[]{:S(2)}) collective-permute-start(f32[1024,128]{1,0:T(8,128)S(1)} %slice.41), channel_id=1, source_target_pairs={{0,1},{1,0},{2,3},{3,2},{4,5},{5,4},{6,7},{7,6},{8,9},{9,8},{10,11... | collective-permute-start | bytes 1572872 | tf_op jit(solution)/shard_map/ppermute | solution.py:379
  23.6 10.3 %collective-permute-start.1 = (f32[256,128]{1,0:T(8,128)S(1)}, f32[256,128]{1,0:T(8,128)S(1)}, u32[]{:S(2)}, u32[]{:S(2)}) collective-permute-start(f32[256,128]{1,0:T(8,128)S(1)} %get-tuple-element.15), channel_id=1, source_target_pairs={{0,4},{1,5},{2,6},{3,7},{4,0},{5,1},{6,2},{7,3},{8,12},{9,13},{10,... | collective-permute-start | bytes 393224 | tf_op jit(solution)/shard_map/ppermute | solution.py:379
  25.4 8.5 %collective-permute-start.2 = (f32[256,128]{1,0:T(8,128)S(1)}, f32[256,128]{1,0:T(8,128)S(1)}, u32[]{:S(2)}, u32[]{:S(2)}) collective-permute-start(f32[256,128]{1,0:T(8,128)S(1)} %get-tuple-element.17), channel_id=1, source_target_pairs={{0,2},{1,3},{2,0},{3,1},{4,6},{5,7},{6,4},{7,5},{8,10},{9,11},{10,... | collective-permute-start | bytes 393224 | tf_op jit(solution)/shard_map/ppermute | solution.py:379
  26.9 14.9 %collective-permute-start.3 = (f32[256,128]{1,0:T(8,128)S(1)}, f32[256,128]{1,0:T(8,128)S(1)}, u32[]{:S(2)}, u32[]{:S(2)}) collective-permute-start(f32[256,128]{1,0:T(8,128)S(1)} %get-tuple-element.16), channel_id=1, source_target_pairs={{0,6},{1,7},{2,4},{3,5},{4,2},{5,3},{6,0},{7,1},{8,14},{9,15},{10,... | collective-permute-start | bytes 393224 | tf_op jit(solution)/shard_map/ppermute | solution.py:379
  41.8 22.0 %collective-permute-start.4 = (f32[64,128]{1,0:T(8,128)S(1)}, f32[64,128]{1,0:T(8,128)S(1)}, u32[]{:S(2)}, u32[]{:S(2)}) collective-permute-start(f32[64,128]{1,0:T(8,128)S(1)} %get-tuple-element.18), channel_id=1, source_target_pairs={{0,16},{1,17},{2,18},{3,19},{4,20},{5,21},{6,22},{7,23},{8,24},{9,... | collective-permute-start | bytes 98312 | tf_op jit(solution)/shard_map/ppermute | solution.py:379
  41.9 21.9 %collective-permute-start.5 = (f32[64,128]{1,0:T(8,128)S(1)}, f32[64,128]{1,0:T(8,128)S(1)}, u32[]{:S(2)}, u32[]{:S(2)}) collective-permute-start(f32[64,128]{1,0:T(8,128)S(1)} %get-tuple-element.20), channel_id=1, source_target_pairs={{0,8},{1,9},{2,10},{3,11},{4,12},{5,13},{6,14},{7,15},{8,0},{9,1},... | collective-permute-start | bytes 98312 | tf_op jit(solution)/shard_map/ppermute | solution.py:379
  43.5 20.2 %collective-permute-start.6 = (f32[64,128]{1,0:T(8,128)S(1)}, f32[64,128]{1,0:T(8,128)S(1)}, u32[]{:S(2)}, u32[]{:S(2)}) collective-permute-start(f32[64,128]{1,0:T(8,128)S(1)} %get-tuple-element.19), channel_id=1, source_target_pairs={{0,24},{1,25},{2,26},{3,27},{4,28},{5,29},{6,30},{7,31},{8,16},{9,... | collective-permute-start | bytes 98312 | tf_op jit(solution)/shard_map/ppermute | solution.py:379
  64.4 6.6 %collective-permute-start.7 = (f32[64,128]{1,0:T(8,128)S(1)}, f32[64,128]{1,0:T(8,128)S(1)}, u32[]{:S(2)}, u32[]{:S(2)}) collective-permute-start(f32[64,128]{1,0:T(8,128)S(1)} %get-tuple-element.9.token_ref.refs_0_), channel_id=1, source_target_pairs={{0,8},{1,9},{2,10},{3,11},{4,12},{5,13},{6,14},{7,15},{8,0},{9,1},... | collective-permute-start | bytes 98312 | tf_op jit(solution)/shard_map/ppermute | solution.py:379
  65.4 5.7 %collective-permute-start.8 = (f32[64,128]{1,0:T(8,128)S(1)}, f32[64,128]{1,0:T(8,128)S(1)}, u32[]{:S(2)}, u32[]{:S(2)}) collective-permute-start(f32[64,128]{1,0:T(8,128)S(1)} %get-tuple-element.9.token_ref.refs_0_), channel_id=1, source_target_pairs={{0,16},{1,17},{2,18},{3,19},{4,20},{5,21},{6,22},{7,23},{8,24},{9,... | collective-permute-start | bytes 98312 | tf_op jit(solution)/shard_map/ppermute | solution.py:379
  66.2 5.7 %collective-permute-start.9 = (f32[64,128]{1,0:T(8,128)S(1)}, f32[64,128]{1,0:T(8,128)S(1)}, u32[]{:S(2)}, u32[]{:S(2)}) collective-permute-start(f32[64,128]{1,0:T(8,128)S(1)} %get-tuple-element.9.token_ref.refs_0_), channel_id=1, source_target_pairs={{0,24},{1,25},{2,26},{3,27},{4,28},{5,29},{6,30},{7,31},{8,16},{9,... | collective-permute-start | bytes 98312 | tf_op jit(solution)/shard_map/ppermute | solution.py:379
  72.1 53.6 %all-to-all-start.1 = ((f32[32,64,256]{2,1,0:T(8,128)}), f32[32,64,256]{2,1,0:T(8,128)S(1)}, u32[]{:S(2)}, u32[]{:S(2)}) async-start(f32[32,64,256]{2,1,0:T(8,128)} %get-tuple-element.10), calls=%async_computation.1 | async-start | bytes 4194304 | tf_op jit(solution)/shard_map/all_to_all | solution.py:412
  76.9 7.8 %collective-permute-start.10 = (f32[64,128]{1,0:T(8,128)S(1)}, f32[64,128]{1,0:T(8,128)S(1)}, u32[]{:S(2)}, u32[]{:S(2)}) collective-permute-start(f32[64,128]{1,0:T(8,128)S(1)} %get-tuple-element.12.refs_0_), channel_id=1, source_target_pairs={{0,2},{1,3},{2,0},{3,1},{4,6},{5,7},{6,4},{7,5},{8,10},{9,11},{10,... | collective-permute-start | bytes 98312 | tf_op jit(solution)/shard_map/ppermute | solution.py:379
  78.7 16.3 %collective-permute-start.11 = (f32[64,128]{1,0:T(8,128)S(1)}, f32[64,128]{1,0:T(8,128)S(1)}, u32[]{:S(2)}, u32[]{:S(2)}) collective-permute-start(f32[64,128]{1,0:T(8,128)S(1)} %get-tuple-element.12.refs_0_), channel_id=1, source_target_pairs={{0,4},{1,5},{2,6},{3,7},{4,0},{5,1},{6,2},{7,3},{8,12},{9,13},{10,... | collective-permute-start | bytes 98312 | tf_op jit(solution)/shard_map/ppermute | solution.py:379
  80.2 14.8 %collective-permute-start.12 = (f32[64,128]{1,0:T(8,128)S(1)}, f32[64,128]{1,0:T(8,128)S(1)}, u32[]{:S(2)}, u32[]{:S(2)}) collective-permute-start(f32[64,128]{1,0:T(8,128)S(1)} %get-tuple-element.12.refs_0_), channel_id=1, source_target_pairs={{0,6},{1,7},{2,4},{3,5},{4,2},{5,3},{6,0},{7,1},{8,14},{9,15},{10,... | collective-permute-start | bytes 98312 | tf_op jit(solution)/shard_map/ppermute | solution.py:379
  95.2 1.3 collective-permute-start.13
where the time goes:
time: 128 us
  waiting for transfers between devices  68 us (53%)
  Pallas kernels  30.2 us (24%)
  starting transfers between devices  28.5 us (22%)
    ppermute x14, waiting for transfers between devices, xor_permute(): lax.ppermute(value, AXES, [(i, i ^ mask) for i in range(device_count)])  50.5 us
    all_to_all x2, waiting for transfers between devices, swap(): return lax.all_to_all(value, AXES, split_axis=0, concat_axis=0, tiled=True)  17.5 us
    ppermute x14, starting transfers between devices, xor_permute(): lax.ppermute(value, AXES, [(i, i ^ mask) for i in range(device_count)])  16.4 us
    all_to_all x2, starting transfers between devices, swap(): return lax.all_to_all(value, AXES, split_axis=0, concat_axis=0, tiled=True)  12.1 us
    pallas_call x1, Pallas kernels, factor_and_solve(): pl.pallas_call(factor_kernel, grid=(1,), in_specs=[whole(value) for value...  11.7 us
    pallas_call x1, Pallas kernels, sampled_terms(): pl.pallas_call(functools.partial(terms_kernel, bits, half), in_specs=[pl....  8.81 us
    pallas_call x1, Pallas kernels, local_mix(): pl.pallas_call(functools.partial(mix_kernel, scale), grid=(cols // GROUP,...  4.63 us
  transfers between devices with their start and end apart: 16, of which 9 were waited for; matrix products, arithmetic and copies ran while one was open for 0% of the time, Pallas kernels for 18%

commit v1 on v0

--- a/solution.py
+++ b/solution.py
@@ -226,7 +226,8 @@
     return whole, error
 
 
-def gram_kernel(scale, terms_ref, picked_ref, gram_ref):
+def gram_kernel(scale, terms_ref, token_ref, picked_ref, gram_ref):
+    del token_ref
     cols = picked_ref.shape[0]
     turned = terms_ref[...].T
     picked = jnp.concatenate([turned[:cols], turned[cols:]], axis=1)
@@ -255,11 +256,11 @@
     gram_ref[...] = jnp.concatenate([high, low], axis=1)
 
 
-def own_gram(terms, cols, per_device, scale):
+def own_gram(terms, cols, per_device, scale, token):
     return pl.pallas_call(
         functools.partial(gram_kernel, scale),
         grid=(1,),
-        in_specs=[whole(terms)],
+        in_specs=[whole(terms), pl.BlockSpec((1, 8, LANES), lambda i: (0, 0, 0))],
         out_specs=(
             pl.BlockSpec((cols, per_device), lambda i: (0, 0)),
             pl.BlockSpec((cols, 2 * cols), lambda i: (0, 0)),
@@ -269,7 +270,7 @@
             jax.ShapeDtypeStruct((cols, 2 * cols), jnp.float32),
         ),
         compiler_params=pltpu.CompilerParams(vmem_limit_bytes=8 << 20),
-    )(terms)
+    )(terms, in_hbm(token))
 
 
 def tree_sum(values):
@@ -418,6 +419,7 @@
     code = sample_offset + odd * rows
     total = sampled_terms(mix, code, me.reshape(1), bits, half)
     for group in in_groups(masks):
+        early = total
         block = total.shape[0] >> len(group)
         mine = total[:block]
         for q in range(1, 1 << len(group)):
@@ -425,8 +427,8 @@
             sent = total[q * block : (q + 1) * block]
             mine = mine + xor_permute(sent, mask, device_count)
         total = mine
-    picked, gram = own_gram(total, cols, per_device, 1.0 / math.sqrt(samples))
-    across = mix_across(received_mix, gram)
+    across = mix_across(received_mix, early)
+    picked, gram = own_gram(total, cols, per_device, 1.0 / math.sqrt(samples), across)
     groups = in_groups(masks)[::-1]
     for number, group in enumerate(groups):
         received = [gram] + [

time: 128 us -> 131 us (1.023)
  waiting for transfers between devices: 68 us -> 70.2 us
    ppermute x14, waiting for transfers between devices: 50.5 us -> 52.7 us  [xor_permute(): lax.ppermute(value, AXES, [(i, i ^ mask) for i in range(device_count)])]
  transfers between devices with their start and end apart: 16 -> 16, of which waited for: 9 -> 10; matrix products, arithmetic and copies ran while one was open for 0% -> 0% of each run, Pallas kernels for 18% -> 16%
where the time goes in v1:
time: 131 us
  waiting for transfers between devices  70.2 us (54%)
  Pallas kernels  30.8 us (24%)
  starting transfers between devices  28.5 us (22%)
    ppermute x14, waiting for transfers between devices, xor_permute(): lax.ppermute(value, AXES, [(i, i ^ mask) for i in range(device_count)])  52.7 us
    all_to_all x2, waiting for transfers between devices, swap(): return lax.all_to_all(value, AXES, split_axis=0, concat_axis=0, tiled=True)  17.5 us
    ppermute x14, starting transfers between devices, xor_permute(): lax.ppermute(value, AXES, [(i, i ^ mask) for i in range(device_count)])  16.4 us
    all_to_all x2, starting transfers between devices, swap(): return lax.all_to_all(value, AXES, split_axis=0, concat_axis=0, tiled=True)  12.1 us
    pallas_call x1, Pallas kernels, factor_and_solve(): pl.pallas_call(factor_kernel, grid=(1,), in_specs=[whole(value) for value...  11.7 us
    pallas_call x1, Pallas kernels, sampled_terms(): pl.pallas_call(functools.partial(terms_kernel, bits, half), in_specs=[pl....  8.81 us
    pallas_call x1, Pallas kernels, local_mix(): pl.pallas_call(functools.partial(mix_kernel, scale), grid=(cols // GROUP,...  4.63 us
  transfers between devices with their start and end apart: 16, of which 10 were waited for; matrix products, arithmetic and copies ran while one was open for 0% of the time, Pallas kernels for 16%

profile of v1, /device:TPU:0, one launch (start us, length us, event | category | flops | bytes accessed | tf_op | source)
XLA Modules:
  0.0 130.5 jit_solution(13395091181955845405)
XLA Ops:
  0.6 4.6 %shard_map.67.far_ref = f32[32,64,256]{2,1,0:T(8,128)} custom-call(f32[64,8192]{1,0:T(8,128)} %panel_ref.1, s32[1,8192]{1,0:T(1,128)} %bitcast.4), custom_call_target="tpu_custom_call" | custom-call | tf_op jit(solution)/shard_map/pallas_call | solution.py:70
  5.3 7.3 %all-to-all-start = ((f32[32,64,256]{2,1,0:T(8,128)}), f32[32,64,256]{2,1,0:T(8,128)S(1)}, u32[]{:S(2)}, u32[]{:S(2)}) async-start(f32[32,64,256]{2,1,0:T(8,128)} %shard_map.67.far_ref), calls=%async_computation | async-start | bytes 4194304 | tf_op jit(solution)/shard_map/all_to_all | solution.py:413
  12.6 8.8 %shard_map.68 = f32[2048,128]{1,0:T(8,128)S(1)} custom-call(s32[4096]{0:T(1024)S(1)} %add.28.code_ref, s32[1]{0:T(128)} %bitcast.1.me_ref, f32[32,64,256]{2,1,0:T(8,128)} %shard_map.67.far_ref), custom_call_target="tpu_custom_call" | custom-call | flops 10485760 | bytes 25165824 | tf_op jit(solution)/shard_map/pallas_call | solution.py:182
  21.8 1.7 %collective-permute-done = f32[1024,128]{1,0:T(8,128)S(1)} collective-permute-done((f32[1024,128]{1,0:T(8,128)S(1)}, f32[1024,128]{1,0:T(8,128)S(1)}, u32[]{:S(2)}, u32[]{:S(2)}) %collective-permute-start) | collective-permute-done | bytes 524320 | tf_op jit(solution)/shard_map/ppermute | solution.py:380
  23.6 1.8 %collective-permute-start.1 = (f32[256,128]{1,0:T(8,128)S(1)}, f32[256,128]{1,0:T(8,128)S(1)}, u32[]{:S(2)}, u32[]{:S(2)}) collective-permute-start(f32[256,128]{1,0:T(8,128)S(1)} %get-tuple-element.15), channel_id=1, source_target_pairs={{0,4},{1,5},{2,6},{3,7},{4,0},{5,1},{6,2},{7,3},{8,12},{9,13},{10,... | collective-permute-start | bytes 393224 | tf_op jit(solution)/shard_map/ppermute | solution.py:380
  25.4 1.5 %collective-permute-start.2 = (f32[256,128]{1,0:T(8,128)S(1)}, f32[256,128]{1,0:T(8,128)S(1)}, u32[]{:S(2)}, u32[]{:S(2)}) collective-permute-start(f32[256,128]{1,0:T(8,128)S(1)} %get-tuple-element.17), channel_id=1, source_target_pairs={{0,2},{1,3},{2,0},{3,1},{4,6},{5,7},{6,4},{7,5},{8,10},{9,11},{10,... | collective-permute-start | bytes 393224 | tf_op jit(solution)/shard_map/ppermute | solution.py:380
  27.1 6.7 %collective-permute-done.1 = f32[256,128]{1,0:T(8,128)S(1)} collective-permute-done((f32[256,128]{1,0:T(8,128)S(1)}, f32[256,128]{1,0:T(8,128)S(1)}, u32[]{:S(2)}, u32[]{:S(2)}) %collective-permute-start.1) | collective-permute-done | bytes 131104 | tf_op jit(solution)/shard_map/ppermute | solution.py:380
  33.9 7.9 %collective-permute-done.3 = f32[256,128]{1,0:T(8,128)S(1)} collective-permute-done((f32[256,128]{1,0:T(8,128)S(1)}, f32[256,128]{1,0:T(8,128)S(1)}, u32[]{:S(2)}, u32[]{:S(2)}) %collective-permute-start.3) | collective-permute-done | bytes 131104 | tf_op jit(solution)/shard_map/ppermute | solution.py:380
  41.9 1.7 %collective-permute-start.5 = (f32[64,128]{1,0:T(8,128)S(1)}, f32[64,128]{1,0:T(8,128)S(1)}, u32[]{:S(2)}, u32[]{:S(2)}) collective-permute-start(f32[64,128]{1,0:T(8,128)S(1)} %get-tuple-element.20), channel_id=1, source_target_pairs={{0,8},{1,9},{2,10},{3,11},{4,12},{5,13},{6,14},{7,15},{8,0},{9,1},... | collective-permute-start | bytes 98312 | tf_op jit(solution)/shard_map/ppermute | solution.py:380
  43.5 2.7 %collective-permute-start.6 = (f32[64,128]{1,0:T(8,128)S(1)}, f32[64,128]{1,0:T(8,128)S(1)}, u32[]{:S(2)}, u32[]{:S(2)}) collective-permute-start(f32[64,128]{1,0:T(8,128)S(1)} %get-tuple-element.19), channel_id=1, source_target_pairs={{0,24},{1,25},{2,26},{3,27},{4,28},{5,29},{6,30},{7,31},{8,16},{9,... | collective-permute-start | bytes 98312 | tf_op jit(solution)/shard_map/ppermute | solution.py:380
  46.3 17.5 %collective-permute-done.4 = f32[64,128]{1,0:T(8,128)S(1)} collective-permute-done((f32[64,128]{1,0:T(8,128)S(1)}, f32[64,128]{1,0:T(8,128)S(1)}, u32[]{:S(2)}, u32[]{:S(2)}) %collective-permute-start.4) | collective-permute-done | bytes 32800 | tf_op jit(solution)/shard_map/ppermute | solution.py:380
  63.8 2.2 %shard_map.69.token_ref.refs_4_ = f32[32,64,256]{2,1,0:T(8,128)} custom-call(f32[32,64,256]{2,1,0:T(8,128)S(1)} %all-to-all-done.in_ref, f32[256,128]{1,0:T(8,128)S(1)} %fusion.1.token_ref), custom_call_target="tpu_custom_call" | custom-call | tf_op jit(solution)/shard_map/pallas_call | solution.py:105
  66.0 1.3 shard_map.70
  69.1 2.6 %collective-permute-start.9 = (f32[64,128]{1,0:T(8,128)S(1)}, f32[64,128]{1,0:T(8,128)S(1)}, u32[]{:S(2)}, u32[]{:S(2)}) collective-permute-start(f32[64,128]{1,0:T(8,128)S(1)} %get-tuple-element.9.refs_0_), channel_id=1, source_target_pairs={{0,24},{1,25},{2,26},{3,27},{4,28},{5,29},{6,30},{7,31},{8,16},{9,... | collective-permute-start | bytes 98312 | tf_op jit(solution)/shard_map/ppermute | solution.py:380
  71.7 2.0 %collective-permute-done.8.refs_2_ = f32[64,128]{1,0:T(8,128)S(1)} collective-permute-done((f32[64,128]{1,0:T(8,128)S(1)}, f32[64,128]{1,0:T(8,128)S(1)}, u32[]{:S(2)}, u32[]{:S(2)}) %collective-permute-start.8) | collective-permute-done | bytes 32800 | tf_op jit(solution)/shard_map/ppermute | solution.py:380
  75.0 4.8 %all-to-all-start.1 = ((f32[32,64,256]{2,1,0:T(8,128)}), f32[32,64,256]{2,1,0:T(8,128)S(1)}, u32[]{:S(2)}, u32[]{:S(2)}) async-start(f32[32,64,256]{2,1,0:T(8,128)} %get-tuple-element.10), calls=%async_computation.1 | async-start | bytes 4194304 | tf_op jit(solution)/shard_map/all_to_all | solution.py:413
  79.8 1.8 %collective-permute-start.10 = (f32[64,128]{1,0:T(8,128)S(1)}, f32[64,128]{1,0:T(8,128)S(1)}, u32[]{:S(2)}, u32[]{:S(2)}) collective-permute-start(f32[64,128]{1,0:T(8,128)S(1)} %get-tuple-element.12.refs_0_), channel_id=1, source_target_pairs={{0,2},{1,3},{2,0},{3,1},{4,6},{5,7},{6,4},{7,5},{8,10},{9,11},{10,... | collective-permute-start | bytes 98312 | tf_op jit(solution)/shard_map/ppermute | solution.py:380
  81.6 1.5 %collective-permute-start.11 = (f32[64,128]{1,0:T(8,128)S(1)}, f32[64,128]{1,0:T(8,128)S(1)}, u32[]{:S(2)}, u32[]{:S(2)}) collective-permute-start(f32[64,128]{1,0:T(8,128)S(1)} %get-tuple-element.12.refs_0_), channel_id=1, source_target_pairs={{0,4},{1,5},{2,6},{3,7},{4,0},{5,1},{6,2},{7,3},{8,12},{9,13},{10,... | collective-permute-start | bytes 98312 | tf_op jit(solution)/shard_map/ppermute | solution.py:380
  83.3 4.3 %collective-permute-done.10.refs_1_ = f32[64,128]{1,0:T(8,128)S(1)} collective-permute-done((f32[64,128]{1,0:T(8,128)S(1)}, f32[64,128]{1,0:T(8,128)S(1)}, u32[]{:S(2)}, u32[]{:S(2)}) %collective-permute-start.10) | collective-permute-done | bytes 32800 | tf_op jit(solution)/shard_map/ppermute | solution.py:380
  87.6 10.3 %collective-permute-done.11.refs_2_ = f32[64,128]{1,0:T(8,128)S(1)} collective-permute-done((f32[64,128]{1,0:T(8,128)S(1)}, f32[64,128]{1,0:T(8,128)S(1)}, u32[]{:S(2)}, u32[]{:S(2)}) %collective-permute-start.11) | collective-permute-done | bytes 32800 | tf_op jit(solution)/shard_map/ppermute | solution.py:380
  98.2 1.2 collective-permute-done.13.refs_1_
  99.4 11.7 %shard_map.74 = (f32[64,64]{1,0:T(8,128)}, f32[64,128]{1,0:T(8,128)}) custom-call(f32[64,128]{1,0:T(8,128)S(1)} %get-tuple-element.11.picked_ref, f32[64,128]{1,0:T(8,128)S(1)} %shard_map.73.refs_0_, f32[64,128]{1,0:T(8,128)S(1)} %collective-permute-done.13.refs_1_), custom_call_target="tpu_custom_call" | custom-call | tf_op jit(solution)/shard_map/pallas_call | solution.py:366
  111.1 17.5 %all-to-all-done.1.in_ref = f32[32,64,256]{2,1,0:T(8,128)S(1)} async-done(((f32[32,64,256]{2,1,0:T(8,128)}), f32[32,64,256]{2,1,0:T(8,128)S(1)}, u32[]{:S(2)}, u32[]{:S(2)}) %all-to-all-start.1) | async-done | bytes 2097184 | tf_op jit(solution)/shard_map/all_to_all | solution.py:413
  128.6 1.9 %shard_map.72 = f32[64,8192]{1,0:T(8,128)} custom-call(f32[32,64,256]{2,1,0:T(8,128)S(1)} %all-to-all-done.1.in_ref), custom_call_target="tpu_custom_call" | custom-call | tf_op jit(solution)/shard_map/pallas_call | solution.py:123
  (28 shorter events, 4.4 us)
Async XLA Ops:
  5.3 7.3 %copy-start.1 = (s32[4096,1]{0,1:T(1,128)S(1)}, s32[4096,1]{0,1:T(1,128)}, u32[]{:S(2)}) copy-start(s32[4096,1]{0,1:T(1,128)} %param.6) | copy-start | bytes 49156
  5.3 7.3 %copy-start = (s32[4096]{0:T(1024)S(1)}, s32[4096]{0:T(1024)}, u32[]{:S(2)}) copy-start(s32[4096]{0:T(1024)} %param.7) | copy-start | bytes 49156
  5.3 58.6 %all-to-all-start = ((f32[32,64,256]{2,1,0:T(8,128)}), f32[32,64,256]{2,1,0:T(8,128)S(1)}, u32[]{:S(2)}, u32[]{:S(2)}) async-start(f32[32,64,256]{2,1,0:T(8,128)} %shard_map.67.far_ref), calls=%async_computation | async-start | bytes 4194304 | tf_op jit(solution)/shard_map/all_to_all | solution.py:413
  21.5 2.0 %collective-permute-start = (f32[1024,128]{1,0:T(8,128)S(1)}, f32[1024,128]{1,0:T(8,128)S(1)}, u32[]{:S(2)}, u32[]{:S(2)}) collective-permute-start(f32[1024,128]{1,0:T(8,128)S(1)} %slice.41), channel_id=1, source_target_pairs={{0,1},{1,0},{2,3},{3,2},{4,5},{5,4},{6,7},{7,6},{8,9},{9,8},{10,11... | collective-permute-start | bytes 1572872 | tf_op jit(solution)/shard_map/ppermute | solution.py:380
  23.6 10.3 %collective-permute-start.1 = (f32[256,128]{1,0:T(8,128)S(1)}, f32[256,128]{1,0:T(8,128)S(1)}, u32[]{:S(2)}, u32[]{:S(2)}) collective-permute-start(f32[256,128]{1,0:T(8,128)S(1)} %get-tuple-element.15), channel_id=1, source_target_pairs={{0,4},{1,5},{2,6},{3,7},{4,0},{5,1},{6,2},{7,3},{8,12},{9,13},{10,... | collective-permute-start | bytes 393224 | tf_op jit(solution)/shard_map/ppermute | solution.py:380
  25.4 8.5 %collective-permute-start.2 = (f32[256,128]{1,0:T(8,128)S(1)}, f32[256,128]{1,0:T(8,128)S(1)}, u32[]{:S(2)}, u32[]{:S(2)}) collective-permute-start(f32[256,128]{1,0:T(8,128)S(1)} %get-tuple-element.17), channel_id=1, source_target_pairs={{0,2},{1,3},{2,0},{3,1},{4,6},{5,7},{6,4},{7,5},{8,10},{9,11},{10,... | collective-permute-start | bytes 393224 | tf_op jit(solution)/shard_map/ppermute | solution.py:380
  26.9 14.9 %collective-permute-start.3 = (f32[256,128]{1,0:T(8,128)S(1)}, f32[256,128]{1,0:T(8,128)S(1)}, u32[]{:S(2)}, u32[]{:S(2)}) collective-permute-start(f32[256,128]{1,0:T(8,128)S(1)} %get-tuple-element.16), channel_id=1, source_target_pairs={{0,6},{1,7},{2,4},{3,5},{4,2},{5,3},{6,0},{7,1},{8,14},{9,15},{10,... | collective-permute-start | bytes 393224 | tf_op jit(solution)/shard_map/ppermute | solution.py:380
  41.8 22.0 %collective-permute-start.4 = (f32[64,128]{1,0:T(8,128)S(1)}, f32[64,128]{1,0:T(8,128)S(1)}, u32[]{:S(2)}, u32[]{:S(2)}) collective-permute-start(f32[64,128]{1,0:T(8,128)S(1)} %get-tuple-element.18), channel_id=1, source_target_pairs={{0,16},{1,17},{2,18},{3,19},{4,20},{5,21},{6,22},{7,23},{8,24},{9,... | collective-permute-start | bytes 98312 | tf_op jit(solution)/shard_map/ppermute | solution.py:380
  41.9 21.9 %collective-permute-start.5 = (f32[64,128]{1,0:T(8,128)S(1)}, f32[64,128]{1,0:T(8,128)S(1)}, u32[]{:S(2)}, u32[]{:S(2)}) collective-permute-start(f32[64,128]{1,0:T(8,128)S(1)} %get-tuple-element.20), channel_id=1, source_target_pairs={{0,8},{1,9},{2,10},{3,11},{4,12},{5,13},{6,14},{7,15},{8,0},{9,1},... | collective-permute-start | bytes 98312 | tf_op jit(solution)/shard_map/ppermute | solution.py:380
  43.5 20.2 %collective-permute-start.6 = (f32[64,128]{1,0:T(8,128)S(1)}, f32[64,128]{1,0:T(8,128)S(1)}, u32[]{:S(2)}, u32[]{:S(2)}) collective-permute-start(f32[64,128]{1,0:T(8,128)S(1)} %get-tuple-element.19), channel_id=1, source_target_pairs={{0,24},{1,25},{2,26},{3,27},{4,28},{5,29},{6,30},{7,31},{8,16},{9,... | collective-permute-start | bytes 98312 | tf_op jit(solution)/shard_map/ppermute | solution.py:380
  67.3 4.5 %collective-permute-start.7 = (f32[64,128]{1,0:T(8,128)S(1)}, f32[64,128]{1,0:T(8,128)S(1)}, u32[]{:S(2)}, u32[]{:S(2)}) collective-permute-start(f32[64,128]{1,0:T(8,128)S(1)} %get-tuple-element.9.refs_0_), channel_id=1, source_target_pairs={{0,8},{1,9},{2,10},{3,11},{4,12},{5,13},{6,14},{7,15},{8,0},{9,1},... | collective-permute-start | bytes 98312 | tf_op jit(solution)/shard_map/ppermute | solution.py:380
  68.2 5.5 %collective-permute-start.8 = (f32[64,128]{1,0:T(8,128)S(1)}, f32[64,128]{1,0:T(8,128)S(1)}, u32[]{:S(2)}, u32[]{:S(2)}) collective-permute-start(f32[64,128]{1,0:T(8,128)S(1)} %get-tuple-element.9.refs_0_), channel_id=1, source_target_pairs={{0,16},{1,17},{2,18},{3,19},{4,20},{5,21},{6,22},{7,23},{8,24},{9,... | collective-permute-start | bytes 98312 | tf_op jit(solution)/shard_map/ppermute | solution.py:380
  69.1 5.7 %collective-permute-start.9 = (f32[64,128]{1,0:T(8,128)S(1)}, f32[64,128]{1,0:T(8,128)S(1)}, u32[]{:S(2)}, u32[]{:S(2)}) collective-permute-start(f32[64,128]{1,0:T(8,128)S(1)} %get-tuple-element.9.refs_0_), channel_id=1, source_target_pairs={{0,24},{1,25},{2,26},{3,27},{4,28},{5,29},{6,30},{7,31},{8,16},{9,... | collective-permute-start | bytes 98312 | tf_op jit(solution)/shard_map/ppermute | solution.py:380
  75.0 53.6 %all-to-all-start.1 = ((f32[32,64,256]{2,1,0:T(8,128)}), f32[32,64,256]{2,1,0:T(8,128)S(1)}, u32[]{:S(2)}, u32[]{:S(2)}) async-start(f32[32,64,256]{2,1,0:T(8,128)} %get-tuple-element.10), calls=%async_computation.1 | async-start | bytes 4194304 | tf_op jit(solution)/shard_map/all_to_all | solution.py:413
  79.8 7.8 %collective-permute-start.10 = (f32[64,128]{1,0:T(8,128)S(1)}, f32[64,128]{1,0:T(8,128)S(1)}, u32[]{:S(2)}, u32[]{:S(2)}) collective-permute-start(f32[64,128]{1,0:T(8,128)S(1)} %get-tuple-element.12.refs_0_), channel_id=1, source_target_pairs={{0,2},{1,3},{2,0},{3,1},{4,6},{5,7},{6,4},{7,5},{8,10},{9,11},{10,... | collective-permute-start | bytes 98312 | tf_op jit(solution)/shard_map/ppermute | solution.py:380
  81.6 16.3 %collective-permute-start.11 = (f32[64,128]{1,0:T(8,128)S(1)}, f32[64,128]{1,0:T(8,128)S(1)}, u32[]{:S(2)}, u32[]{:S(2)}) collective-permute-start(f32[64,128]{1,0:T(8,128)S(1)} %get-tuple-element.12.refs_0_), channel_id=1, source_target_pairs={{0,4},{1,5},{2,6},{3,7},{4,0},{5,1},{6,2},{7,3},{8,12},{9,13},{10,... | collective-permute-start | bytes 98312 | tf_op jit(solution)/shard_map/ppermute | solution.py:380
  83.1 14.8 %collective-permute-start.12 = (f32[64,128]{1,0:T(8,128)S(1)}, f32[64,128]{1,0:T(8,128)S(1)}, u32[]{:S(2)}, u32[]{:S(2)}) collective-permute-start(f32[64,128]{1,0:T(8,128)S(1)} %get-tuple-element.12.refs_0_), channel_id=1, source_target_pairs={{0,6},{1,7},{2,4},{3,5},{4,2},{5,3},{6,0},{7,1},{8,14},{9,15},{10,... | collective-permute-start | bytes 98312 | tf_op jit(solution)/shard_map/ppermute | solution.py:380
  98.1 1.3 collective-permute-start.13
